TPU v7x, 256 devices: a whole 4x4x8 slice. The times are simulated.
256 devices in a mesh: tgt: 64 (over z, y, core), src: 4 (over x).
Axes of the slice: x: 4, y: 4, z: 8, core: 2. Of those that a mesh axis runs over, the one named last changes fastest.
Arguments:
- tgt_coords: bfloat16 [3, 262144], P(None, 'tgt'), may hold values from -1 to 1
- tgt_embed: bfloat16 [64, 262144], P(None, 'tgt'), may hold values from -3 to 3
- tile_perm: int32 [512], P('tgt'), may hold values from 0 to 511, each once
- tile_count: int32 [512], replicated, may hold values from 1 to 512, as said below
- src_coords: bfloat16 [3, 32768], P(None, ('tgt', 'src')), may hold values from -1 to 1
- src_embed: bfloat16 [64, 32768], P(None, ('tgt', 'src')), may hold values from -3 to 3
- anchors: float32 [3, 256], replicated, may hold values from -1 to 1
- sigma2: float32 [1], replicated, may hold values from 0.2 to 1
- outlier_weight: float32 [1], replicated, may hold values from 0.1 to 0.5
- warp_lambda: float32 [1], replicated, may hold values from 0.05 to 0.5
Outputs:
- warped: float32 [3, 32768], P(None, ('tgt', 'src'))
- masses: float32 [32768], P(('tgt', 'src'))
Inputs may be any that keep to these rules, and one draw needn't show every extreme that they name: `tile_count`: one spatial tile has all 512 cells valid.
All inputs are finite; a program needn't handle non-finite values.
Results may differ from a plain program's by a relative error of at most 0.0003.
Values may be sent and summed in bfloat16 or wider, within the bound.
No kernel may reach another device: no remote copies, remote signals or barrier semaphores. Data moves between devices by JAX's collectives and lax.ppermute only.
A program may use at most 64 MiB of HBM per device.

v0:
```python
import jax
import jax.numpy as jnp
from jax import lax
from jax.sharding import PartitionSpec as P

TILE = 512


SCORE_GAIN = 4.0
ANCHOR_WIDTH = 0.1


def cell_mask(tile_perm, tile_count):
    tiles_all = tile_count.shape[0]
    hits = tile_perm[:, None] == jnp.arange(tiles_all, dtype=jnp.int32)[None, :]
    counts = jnp.sum(jnp.where(hits, tile_count[None, :], 0), axis=1)
    within = jnp.arange(TILE, dtype=jnp.int32)
    return (within[None, :] < counts[:, None]).astype(jnp.float32).reshape(-1)


def squared_gap(first, second):
    gap_a = first[0][:, None] - second[0][None, :]
    gap_b = first[1][:, None] - second[1][None, :]
    gap_c = first[2][:, None] - second[2][None, :]
    return gap_a * gap_a + gap_b * gap_b + gap_c * gap_c


def affinity(src_xyz, src_feat, tgt_xyz, tgt_feat, keep, inv_spread):
    similar = lax.dot_general(
        src_feat, tgt_feat, (((0,), (0,)), ((), ())), preferred_element_type=jnp.float32
    )
    scale = SCORE_GAIN / src_feat.shape[0]
    return jnp.exp(similar * scale - squared_gap(src_xyz, tgt_xyz) * inv_spread) * keep[None, :]


def moments(posterior, tgt_xyz):
    weights = jnp.concatenate([jnp.ones_like(tgt_xyz[:1]), tgt_xyz], axis=0)
    return lax.dot_general(
        weights,
        posterior,
        (((1,), (1,)), ((), ())),
        precision=lax.Precision.HIGHEST,
        preferred_element_type=jnp.float32,
    )


def warp_terms(src_xyz, anchors, masses, moved):
    basis = jnp.exp(-squared_gap(src_xyz, anchors) * (0.5 / ANCHOR_WIDTH))
    gram = lax.dot_general(
        basis,
        masses[:, None] * basis,
        (((0,), (0,)), ((), ())),
        precision=lax.Precision.HIGHEST,
        preferred_element_type=jnp.float32,
    )
    pulled = jnp.dot(moved - masses[None, :] * src_xyz, basis, precision=lax.Precision.HIGHEST)
    return (basis, gram, pulled, jnp.sum(masses))


def warp_solve(basis, gram, pulled, total, anchors, sigma2, warp_lambda):
    anchor_gram = jnp.exp(-squared_gap(anchors, anchors) * (0.5 / ANCHOR_WIDTH))
    system = gram / total + warp_lambda[0] * sigma2[0] * (
        anchor_gram + jnp.eye(anchors.shape[1], dtype=jnp.float32)
    )
    factor = jnp.linalg.cholesky(system)
    coeffs = jax.scipy.linalg.cho_solve((factor, True), (pulled / total).T)
    return lax.dot_general(
        coeffs,
        basis,
        (((0,), (1,)), ((), ())),
        precision=lax.Precision.HIGHEST,
        preferred_element_type=jnp.float32,
    )


def split_blocks(tgt_xyz, tgt_feat, keep, width):
    count = tgt_xyz.shape[1] // width
    channels = tgt_feat.shape[0]
    xyz_blocks = tgt_xyz.reshape(3, count, width).transpose(1, 0, 2)
    feat_blocks = tgt_feat.reshape(channels, count, width).transpose(1, 0, 2)
    return (xyz_blocks, feat_blocks, keep.reshape(count, width))


def local(
    tgt_coords,
    tgt_embed,
    tile_perm,
    tile_count,
    src_coords,
    src_embed,
    anchors,
    sigma2,
    outlier_weight,
    warp_lambda,
):
    keep_all = cell_mask(tile_perm, tile_count)
    inv_spread = 0.5 / sigma2[0]
    total_sources = src_coords.shape[1] * lax.axis_size("tgt") * lax.axis_size("src")
    floor_term = outlier_weight[0] / (1.0 - outlier_weight[0]) * total_sources
    tgt_xyz_all = tgt_coords.astype(jnp.float32)
    cells = tgt_xyz_all.shape[1]
    panel_xyz, panel_feat = (
        lax.all_gather(src_coords, "tgt", axis=1, tiled=True),
        lax.all_gather(src_embed, "tgt", axis=1, tiled=True),
    )
    panel_xyz = panel_xyz.astype(jnp.float32)
    xyz_blocks, feat_blocks, keep_blocks = split_blocks(
        tgt_xyz_all, tgt_embed, keep_all, min(256, cells)
    )

    def partial_sum(item):
        xyz, feat, keep = item
        return jnp.sum(affinity(panel_xyz, panel_feat, xyz, feat, keep, inv_spread), axis=0)

    partial_value = lax.map(partial_sum, (xyz_blocks, feat_blocks, keep_blocks))
    normals = lax.psum(partial_value, "src") + floor_term

    def visit(carry, item):
        xyz, feat, keep, normal = item
        kernel = affinity(panel_xyz, panel_feat, xyz, feat, keep, inv_spread)
        return (carry + moments(kernel / normal[None, :], xyz), None)

    sums, unused = lax.scan(
        visit,
        jnp.zeros((4, panel_xyz.shape[1]), jnp.float32),
        (xyz_blocks, feat_blocks, keep_blocks, normals),
    )
    owned = lax.psum_scatter(sums, "tgt", scatter_dimension=1, tiled=True)
    masses = owned[0]
    src_xyz = src_coords.astype(jnp.float32)
    basis, gram, pulled, total = warp_terms(src_xyz, anchors, masses, owned[1:])
    gram, pulled, total = lax.psum((gram, pulled, total), ("tgt", "src"))
    shift = warp_solve(basis, gram, pulled, total, anchors, sigma2, warp_lambda)
    return (src_xyz + shift, masses)


def solution(mesh):
    placed = (
        P(None, "tgt"),
        P(None, "tgt"),
        P("tgt"),
        P(),
        P(None, ("tgt", "src")),
        P(None, ("tgt", "src")),
        P(),
        P(),
        P(),
        P(),
    )
    return jax.shard_map(
        local,
        mesh=mesh,
        in_specs=placed,
        out_specs=(P(None, ("tgt", "src")), P(("tgt", "src"))),
        check_vma=False,
    )
```

profile of v0, /device:TPU:1, one launch (start us, length us, event | category | flops | bytes accessed | tf_op | source)
XLA Modules:
  0.0 925.4 jit_solution(12478259403595993677)
XLA Ops:
  10.6 48.4 %all_gather.7 = bf16[3,8192]{1,0:T(4,128)(2,1)S(1)} all-gather(bf16[3,128]{1,0:T(4,128)(2,1)} %param.18), channel_id=1, replica_groups=mesh['tgt'=64,'src'=4] {'tgt'}, dimensions={1}, use_global_device_ids=true | all-gather | bytes 49920 | tf_op jit(solution)/shard_map/all_gather | solution.py:103
  63.2 22.1 %all-gather.2.cloned.1.call-done = bf16[64,8192]{1,0:T(8,128)(2,1)} async-done(((bf16[64,128]{1,0:T(8,128)(2,1)}), bf16[64,8192]{1,0:T(8,128)(2,1)}) %all-gather.2.cloned.1.call-update) | async-done | bytes 1048592 | tf_op jit(solution)/shard_map/all_gather | solution.py:104
  85.3 103.0 %while.22 = (s32[]{:T(128)}, f32[16,256]{1,0:T(8,128)S(1)}, bf16[16,64,256]{2,1,0:T(8,128)(2,1)S(1)}, bf16[64,8192]{1,0:T(8,128)(2,1)}, f32[3,8192]{1,0:T(4,128)...) while((s32[]{:T(128)}, f32[16,256]{1,0:T(8,128)S(1)}, ...), condition=%wide.region_3.4_spmd, body=%wide.region_1.3_spmd.sunk | while | flops 295698176 | bytes 1391785 | solution.py:115
  98.3 6.3 fusion.93
  104.7 6.3 fusion.93
  111.2 6.3 fusion.93
  124.1 6.3 fusion.93
  188.4 13.0 %psum.28 = f32[16,256]{1,0:T(8,128)S(1)} all-reduce(f32[16,256]{1,0:T(8,128)S(1)} %get-tuple-element.91), channel_id=1, replica_groups=mesh['tgt'=64,'src'=4] {'src'}, use_global_device_ids=true, to_apply=%region_4.5 | all-reduce | flops 4096 | bytes 32768 | tf_op jit(solution)/shard_map/psum | solution.py:116
  201.3 251.3 %while.24 = (s32[]{:T(128)}, f32[4,8192]{1,0:T(4,128)S(1)}, f32[16,3,256]{2,1,0:T(4,128)S(1)}, bf16[16,64,256]{2,1,0:T(8,128)(2,1)S(1)}, bf16[64,8192]{1,0:T(8,1...) while((s32[]{:T(128)}, f32[4,8192]{1,0:T(4,128)S(1)}, ...), condition=%wide.region_6.7_spmd.clone, body=%wide.region_5.6_spmd.clone.sunk | while | flops 396427264 | bytes 18440380 | solution.py:123
  201.5 8.1 fusion.100
  209.6 7.4 convolution_add_fusion.3
  217.2 8.2 fusion.100
  225.3 7.4 convolution_add_fusion.3
  232.9 8.2 fusion.100
  241.0 7.4 convolution_add_fusion.3
  248.6 8.2 fusion.100
  256.7 7.4 convolution_add_fusion.3
  264.3 8.2 fusion.100
  272.4 7.4 convolution_add_fusion.3
  280.0 8.2 fusion.100
  288.1 7.4 convolution_add_fusion.3
  295.7 8.2 fusion.100
  303.9 7.4 convolution_add_fusion.3
  311.4 8.2 fusion.100
  319.6 7.4 convolution_add_fusion.3
  327.1 8.2 fusion.100
  335.3 7.4 convolution_add_fusion.3
  342.8 8.2 fusion.100
  351.0 7.4 convolution_add_fusion.3
  358.5 8.2 fusion.100
  366.7 7.4 convolution_add_fusion.3
  374.2 8.2 fusion.100
  382.4 7.4 convolution_add_fusion.3
  389.9 8.2 fusion.100
  398.1 7.4 convolution_add_fusion.3
  405.6 8.2 fusion.100
  413.8 7.4 convolution_add_fusion.3
  421.3 8.2 fusion.100
  429.5 7.4 convolution_add_fusion.3
  437.0 8.2 fusion.100
  445.2 7.4 convolution_add_fusion.3
  455.3 139.3 %reduce-scatter.4.cloned.1.call-done = f32[128,4]{1,0:T(8,128)} async-done(((f32[8192,4]{1,0:T(8,128)}), f32[128,4]{1,0:T(8,128)}) %reduce-scatter.4.cloned.1.call-update) | async-done | bytes 2064
  598.8 79.8 %all-reduce.2 = (f32[]{:T(128)}, f32[3,256]{1,0:T(4,128)S(1)}) all-reduce(f32[]{:T(128)} %get-tuple-element.246, f32[3,256]{1,0:T(4,128)S(1)} %fusion.21), channel_id=1, replica_groups=mesh['tgt'=64,'src'=4] {'tgt','src'}, use_global_device_ids=true, to_apply=%region_10.11 | all-reduce | flops 769 | bytes 6152 | tf_op jit(solution)/shard_map/psum | solution.py:132
  679.2 174.1 %all-reduce.5.cloned.1.call-done = f32[256,256]{0,1:T(8,128)} async-done(((f32[256,256]{0,1:T(8,128)}), f32[256,256]{0,1:T(8,128)}) %all-reduce.5.cloned.1.call-update) | async-done | bytes 262160 | tf_op jit(solution)/shard_map/psum | solution.py:132
  856.9 11.7 %cholesky.50 = f32[128,128]{1,0:T(8,128)S(1)} custom-call(f32[128,128]{1,0:T(8,128)S(1)} %cholesky.118), custom_call_target="Cholesky" | custom-call | tf_op jit(solution)/shard_map/jit(cholesky)/cholesky | solution.py:65
  868.7 9.8 %custom-call.18 = f32[1,128,128]{1,2,0:T(8,128)S(1)} custom-call(f32[1,128,128]{2,1,0:T(8,128)S(1)} %get-tuple-element.245), custom_call_target="InvertDiagBlocksLowerTriangular" | custom-call | tf_op jit(solution)/shard_map/jit(cholesky)/cholesky | solution.py:65
  879.0 11.7 %cholesky.105 = f32[128,128]{1,0:T(8,128)S(1)} custom-call(f32[128,128]{1,0:T(8,128)S(1)} %convolution_subtract_fusion), custom_call_target="Cholesky" | custom-call | tf_op jit(solution)/shard_map/jit(cholesky)/cholesky | solution.py:65
  896.9 19.9 %custom-call.19 = f32[2,128,128]{1,2,0:T(8,128)S(1)} custom-call(f32[2,128,128]{2,1,0:T(8,128)S(1)} %get-tuple-element.100), custom_call_target="InvertDiagBlocksLowerTriangular" | custom-call | tf_op jit(solution)/shard_map/jit(_cho_solve)/triangular_solve | solution.py:66
  (203 shorter events, 106.8 us)
Async XLA Ops:
  7.2 78.1 %all-gather.2.cloned.1.call-start = ((), (), s32[]{:S(2)}) async-start(), calls=%async_computation.1 | async-start | bytes 1064960 | tf_op jit(solution)/shard_map/all_gather | solution.py:104
  7.9 586.7 %reduce-scatter.4.cloned.1.call-start = ((), (), s32[]{:S(2)}) async-start(), calls=%async_computation.3 | async-start | bytes 4259840
  452.6 145.9 %copy-start = (bf16[3,128]{1,0:T(4,128)(2,1)S(1)}, bf16[3,128]{1,0:T(4,128)(2,1)}, u32[]{:S(2)}) copy-start(bf16[3,128]{1,0:T(4,128)(2,1)} %param.18) | copy-start | bytes 2308
  455.3 398.0 %all-reduce.5.cloned.1.call-start = ((), (), s32[]{:S(2)}) async-start(), calls=%async_computation.2 | async-start | bytes 524288 | tf_op jit(solution)/shard_map/psum | solution.py:132
  597.1 321.8 %copy-start.1 = (f32[1,128]{1,0:T(1,128)}, f32[1,128]{1,0:T(1,128)S(1)}, u32[]{:S(2)}) copy-start(f32[1,128]{1,0:T(1,128)S(1)} %copy.29) | copy-start | bytes 1540
Sparse Core Ops, SparseCore 0:
  10.6 74.6 all-gather.1
  455.4 139.1 reduce-scatter.3
  600.9 252.3 all-reduce.4
where the time goes:
time: 928 us; the launch traced here: 925 us
  matrix products  354 us (38%)
  waiting for transfers between devices  336 us (36%)
  blocking collectives  141 us (15%)
  other arithmetic  61.9 us (7%)
  between operations  17.2 us (2%)
  local copies, waits for them, and re-layouts  13.9 us (1%)
    dot_general x32, matrix products, affinity(): lax.dot_general(src_feat, tgt_feat, (((0,), (0,)), ((), ())), preferred_e...  231 us
    psum x1, waiting for transfers between devices, local(): gram, pulled, total = lax.psum((gram, pulled, total), ('tgt', 'src'))  174 us
    unnamed x4, waiting for transfers between devices  140 us
    dot_general x16, matrix products, moments(): lax.dot_general(weights, posterior, (((1,), (1,)), ((), ())), precision=l...  119 us
    psum x1, blocking collectives, local(): gram, pulled, total = lax.psum((gram, pulled, total), ('tgt', 'src'))  79.8 us
    all_gather x1, blocking collectives, local(): lax.all_gather(src_coords, 'tgt', axis=1, tiled=True)  48.4 us
    another operation x6, other arithmetic, warp_solve(): factor = jnp.linalg.cholesky(system)  34 us
    all_gather x1, waiting for transfers between devices, local(): lax.all_gather(src_embed, 'tgt', axis=1, tiled=True)  22.1 us
  transfers between devices with their start and end apart: 3, of which 3 were waited for; matrix products, arithmetic and copies ran while one was open for 1% of the time, Pallas kernels for 0%

commit v1 on v0

v1 whole, which is shorter than its diff:
```python
import functools
import math

import jax
import jax.numpy as jnp
from jax import lax
from jax.experimental import pallas as pl
from jax.experimental.pallas import tpu as pltpu
from jax.sharding import Mesh
from jax.sharding import PartitionSpec as P

TILE = 512
SCORE_GAIN = 4.0
ANCHOR_WIDTH = 0.1
LOG2E = math.log2(math.e)

ROWS = 256
LANES = 128
DEPTH = 256
STORED = 14
MASKED = -30000.0
HALF = 232
WARP_ROWS = 200

F32 = jnp.float32
BF16 = jnp.bfloat16
WHOLE = pl.BlockSpec(memory_space=pltpu.VMEM)
SCALAR = pl.BlockSpec(memory_space=pltpu.SMEM)


def split3(value):
    high = value.astype(BF16).astype(F32)
    rest = value - high
    middle = rest.astype(BF16).astype(F32)
    return high, middle, rest - middle


def pick_rows(rows, count):
    width = rows[0].shape[1]
    place = lax.broadcasted_iota(jnp.int32, (count, width), 0)
    out = jnp.zeros((count, width), F32)
    for index, row in enumerate(rows):
        out = jnp.where(place == index, row, out)
    return out


def prepare_targets(perm_ref, count_ref, sigma2_ref, xyz_ref, feat_ref, out_ref, blocks_ref):
    inv = (0.5 * LOG2E) / jnp.full((1, TILE), sigma2_ref[0], F32)
    tiles = perm_ref.shape[0]
    offset = jnp.int32(0)
    one = jnp.ones((1, TILE), F32)
    lane = lax.broadcasted_iota(jnp.int32, (1, TILE), 1)
    for tile in range(tiles):
        span = slice(tile * TILE, (tile + 1) * TILE)
        count = count_ref[perm_ref[tile]]
        xyz = xyz_ref[:, span].astype(F32)
        x0, x1, x2 = xyz[0:1], xyz[1:2], xyz[2:3]
        square = -(x0 * x0 + x1 * x1 + x2 * x2) * inv
        qh, qm, ql = split3(jnp.where(lane < count, square, MASKED))
        side = pick_rows([x0, x1, x2, one, x0, x1, x2, one, x0, x1, x2, one, qh, qm, ql], 16)
        feat = feat_ref[:, span].astype(F32)
        wide = jnp.concatenate([feat, side, jnp.zeros((48, TILE), F32), feat, feat], axis=0)
        out_ref[pl.ds(pl.multiple_of(offset, 16), TILE), :] = wide.T.astype(BF16)
        offset = offset + ((count + 15) // 16) * 16
    blank = jnp.where(lax.broadcasted_iota(jnp.int32, (ROWS, DEPTH), 1) == 76, MASKED, 0.0)
    out_ref[pl.ds(pl.multiple_of(offset, 16), ROWS), :] = blank.astype(BF16)
    blocks_ref[0] = (offset + ROWS - 1) // ROWS


def widen_sources(sigma2_ref, panel_ref, wide_ref):
    gain = SCORE_GAIN / 64 * LOG2E
    inv = (0.5 * LOG2E) / jnp.full((1, LANES), sigma2_ref[0], F32)
    one = jnp.ones((1, LANES), F32)

    def piece(index, unused):
        at = pl.ds(pl.multiple_of(index * LANES, LANES), LANES)
        both = panel_ref[index].astype(F32)
        high, middle, low = split3(both[0:64] * gain)
        y0, y1, y2 = both[64:65], both[65:66], both[66:67]
        square = -(y0 * y0 + y1 * y1 + y2 * y2) * inv
        parts = [split3(row) for row in (y0 * (2.0 * inv), y1 * (2.0 * inv), y2 * (2.0 * inv), square)]
        rows = [part[level] for level in range(3) for part in parts] + [one, one, one]
        wide_ref[0:64, at] = high.astype(BF16)
        wide_ref[64:80, at] = pick_rows(rows, 16).astype(BF16)
        wide_ref[80:128, at] = jnp.zeros((48, LANES), BF16)
        wide_ref[128:192, at] = middle.astype(BF16)
        wide_ref[192:256, at] = low.astype(BF16)
        return unused

    lax.fori_loop(0, panel_ref.shape[0], piece, 0)


def kernel_pass(blocks_ref, sigma2_ref, tgt_ref, panel_ref, kernel_ref, sum_ref, wide_ref):
    step = pl.program_id(0)

    @pl.when(step == 0)
    def _():
        widen_sources(sigma2_ref, panel_ref, wide_ref)

    def block(store):
        tgt = tgt_ref[...]
        total = jnp.zeros((ROWS, LANES), F32)
        for start in range(0, wide_ref.shape[1], 256):
            score = jnp.dot(tgt, wide_ref[:, start : start + 256], preferred_element_type=F32)
            value = jnp.exp2(score)
            rounded = value.astype(BF16)
            if store:
                kernel_ref[:, start : start + 256] = rounded
            value = rounded.astype(F32)
            total += value[:, 0:128] + value[:, 128:256]
        sum_ref[pl.ds(step, 1), :] = jnp.sum(total.T, axis=0, keepdims=True)

    blocks = blocks_ref[0]

    @pl.when((step < STORED) & (step < blocks))
    def _():
        block(True)

    @pl.when((step >= STORED) & (step < blocks))
    def _():
        block(False)


def warp_sums(acc_ref, panel_ref, anchors_ref, core_ref, out_ref, side_ref, gram_ref):
    pieces = panel_ref.shape[0]
    sources = pieces * LANES
    count = anchors_ref.shape[1]
    rate = 0.5 / ANCHOR_WIDTH * LOG2E
    one = jnp.ones((1, LANES), F32)

    def piece(index, unused):
        at = pl.ds(pl.multiple_of(index * LANES, LANES), LANES)
        y = panel_ref[index, 64:80, :].astype(F32)
        y0, y1, y2 = y[0:1], y[1:2], y[2:3]
        rh, rm, rl = split3(-(y0 * y0 + y1 * y1 + y2 * y2) * rate)
        rows = [y0, y1, y2, one, y0, y1, y2, one, y0, y1, y2, one, rh, rm, rl]
        side_ref[:, at] = pick_rows(rows, 16).astype(BF16)
        return unused

    lax.fori_loop(0, pieces, piece, 0)
    a0, a1, a2 = anchors_ref[0:1, :], anchors_ref[1:2, :], anchors_ref[2:3, :]
    square = -(a0 * a0 + a1 * a1 + a2 * a2) * rate
    parts = [split3(row) for row in (a0 * (2.0 * rate), a1 * (2.0 * rate), a2 * (2.0 * rate), square)]
    ones = jnp.ones((1, count), F32)
    rows = [part[level] for level in range(3) for part in parts] + [ones, ones, ones]
    anchor_side = pick_rows(rows, LANES).T.astype(BF16)[:, 0:16]
    sums = acc_ref[...]
    sums = sums + pltpu.roll(sums, 4, 0)
    acc_ref[...] = sums
    gram_ref[...] = jnp.zeros_like(gram_ref)
    width = 512

    def chunk(index, unused):
        at = pl.ds(pl.multiple_of(index * width, width), width)
        side = side_ref[:, at]
        basis = jnp.exp2(jnp.dot(anchor_side, side, preferred_element_type=F32))
        moment = acc_ref[:, at]
        mass = moment[3:4, :]
        pull = moment - mass * side.astype(F32)[0:8]
        left = jnp.concatenate([basis * mass, pull, jnp.zeros_like(pull)], axis=0)
        left_high = left.astype(BF16)
        left_low = (left - left_high.astype(F32)).astype(BF16)
        basis_high = basis.astype(BF16)
        basis_low = (basis - basis_high.astype(F32)).astype(BF16)
        last = (((1,), (1,)), ((), ()))
        first = lax.dot_general(
            jnp.concatenate([left_high, left_low], axis=0), basis_high, last, preferred_element_type=F32
        )
        second = lax.dot_general(left_high, basis_low, last, preferred_element_type=F32)
        gram_ref[...] += first[0:272] + first[272:544] + second
        return unused

    lax.fori_loop(0, sources // width, chunk, 0)
    total = jnp.sum(acc_ref[3:4, :])
    row = lax.broadcasted_iota(jnp.int32, (8, LANES), 0)
    core = core_ref[0]
    for half in range(2):
        at = jnp.where(core == half, 0, 1)
        if half == 0:
            out_ref[at, 0:128, :] = gram_ref[0:128, 0:128]
            out_ref[at, 128:192, :] = gram_ref[0:64, 128:256]
        else:
            out_ref[at, 0:64, :] = gram_ref[64:128, 128:256]
            out_ref[at, 64:192, :] = gram_ref[128:256, 128:256]
        pulled = gram_ref[256:264, half * LANES : (half + 1) * LANES]
        out_ref[at, 192:200, :] = jnp.where(row == 3, total, pulled)
        for r in range(32):
            s = (half * 32 + r) * LANES
            out_ref[at, 200 + r : 201 + r, :] = acc_ref[3:4, s : s + LANES]


def moment_pass(
    blocks_ref, sigma2_ref, outlier_ref, core_ref, sum_ref, tgt_ref, kernel_ref, panel_ref, anchors_ref,
    out_ref, wide_ref, acc_ref, side_ref, gram_ref, *, total_sources,
):
    step = pl.program_id(0)

    @pl.when(step == 0)
    def _():
        acc_ref[...] = jnp.zeros_like(acc_ref)

    outlier = jnp.full((1, ROWS), outlier_ref[0], F32)
    floor = outlier / (1.0 - outlier) * total_sources
    normal = jnp.sum(sum_ref[:, pl.ds(step, 1), :], axis=0) + floor
    side = tgt_ref[:, 0:128].astype(F32).T[64:72]
    weight = side / normal
    high = weight.astype(BF16).astype(F32)
    row = lax.broadcasted_iota(jnp.int32, weight.shape, 0)
    weight = jnp.where(row < 4, high, weight - high).astype(BF16)

    blocks = blocks_ref[0]

    @pl.when((step < STORED) & (step < blocks))
    def _():
        for start in range(0, kernel_ref.shape[1], 1024):
            at = slice(start, start + 1024)
            acc_ref[:, at] += jnp.dot(weight, kernel_ref[:, at], preferred_element_type=F32)

    @pl.when((step == STORED) & (step < blocks))
    def _():
        widen_sources(sigma2_ref, panel_ref, wide_ref)

    @pl.when((step >= STORED) & (step < blocks))
    def _():
        for start in range(0, wide_ref.shape[1], 512):
            at = slice(start, start + 512)
            score = jnp.dot(tgt_ref[...], wide_ref[:, at], preferred_element_type=F32)
            value = jnp.exp2(score).astype(BF16)
            acc_ref[:, at] += jnp.dot(weight, value, preferred_element_type=F32)

    @pl.when(step == blocks - 1)
    def _():
        warp_sums(acc_ref, panel_ref, anchors_ref, core_ref, out_ref, side_ref, gram_ref)


def squared_gap(first, second):
    gap_a = first[0][:, None] - second[0][None, :]
    gap_b = first[1][:, None] - second[1][None, :]
    gap_c = first[2][:, None] - second[2][None, :]
    return gap_a * gap_a + gap_b * gap_b + gap_c * gap_c


def warp_solve(basis, gram, pulled, total, anchors, sigma2, warp_lambda):
    anchor_gram = jnp.exp(-squared_gap(anchors, anchors) * (0.5 / ANCHOR_WIDTH))
    system = gram / total + warp_lambda[0] * sigma2[0] * (
        anchor_gram + jnp.eye(anchors.shape[1], dtype=F32)
    )
    factor = jnp.linalg.cholesky(system)
    coeffs = jax.scipy.linalg.cho_solve((factor, True), (pulled / total).T)
    return lax.dot_general(
        coeffs, basis, (((0,), (1,)), ((), ())),
        precision=lax.Precision.HIGHEST, preferred_element_type=F32,
    )


def gather(value, axis):
    return lax.all_gather(value, axis, axis=0, tiled=True)


def local(
    tgt_coords, tgt_embed, tile_perm, tile_count, src_coords, src_embed, anchors, sigma2,
    outlier_weight, warp_lambda,
):
    cells = tgt_coords.shape[1]
    zs, ys, cs, xs = (lax.axis_size(name) for name in ("z", "y", "c", "x"))
    pieces = zs * ys * cs
    sources = pieces * LANES
    blocks_max = cells // ROWS

    own = jnp.concatenate([src_embed, src_coords, jnp.zeros((13, LANES), BF16)], axis=0)[None]
    panel = gather(gather(gather(own, "y"), "z"), "c")

    targets, blocks = pl.pallas_call(
        prepare_targets,
        in_specs=[SCALAR, SCALAR, SCALAR, WHOLE, WHOLE],
        out_specs=[WHOLE, SCALAR],
        out_shape=[
            jax.ShapeDtypeStruct((cells + TILE, DEPTH), BF16),
            jax.ShapeDtypeStruct((1,), jnp.int32),
        ],
        name="prepare_targets",
    )(tile_perm, tile_count, sigma2, tgt_coords, tgt_embed)

    def at_block(i, b):
        return jnp.minimum(i, b[0] - 1), 0

    def at_stored(i, b):
        return jnp.minimum(jnp.minimum(i, b[0] - 1), STORED - 1), 0

    kernel, sums = pl.pallas_call(
        kernel_pass,
        grid_spec=pltpu.PrefetchScalarGridSpec(
            num_scalar_prefetch=1,
            grid=(blocks_max,),
            in_specs=[
                SCALAR,
                pl.BlockSpec((ROWS, DEPTH), at_block),
                pl.BlockSpec((pieces, 80, LANES), lambda i, b: (0, 0, 0)),
            ],
            out_specs=[
                pl.BlockSpec((ROWS, sources), at_stored),
                pl.BlockSpec((blocks_max, ROWS), lambda i, b: (0, 0)),
            ],
            scratch_shapes=[pltpu.VMEM((DEPTH, sources), BF16)],
        ),
        out_shape=[
            jax.ShapeDtypeStruct((STORED * ROWS, sources), BF16),
            jax.ShapeDtypeStruct((blocks_max, ROWS), F32),
        ],
        compiler_params=pltpu.CompilerParams(vmem_limit_bytes=40 << 20),
        name="kernel_pass",
    )(blocks, sigma2, targets, panel)

    all_sums = gather(sums[None], "x")

    core = lax.axis_index("c").astype(jnp.int32)[None]
    share = pl.pallas_call(
        functools.partial(moment_pass, total_sources=sources * xs),
        grid_spec=pltpu.PrefetchScalarGridSpec(
            num_scalar_prefetch=1,
            grid=(blocks_max,),
            in_specs=[
                SCALAR,
                SCALAR,
                SCALAR,
                pl.BlockSpec((xs, blocks_max, ROWS), lambda i, b: (0, 0, 0)),
                pl.BlockSpec((ROWS, DEPTH), at_block),
                pl.BlockSpec((ROWS, sources), at_stored),
                pl.BlockSpec((pieces, 80, LANES), lambda i, b: (0, 0, 0)),
                pl.BlockSpec((3, 256), lambda i, b: (0, 0)),
            ],
            out_specs=pl.BlockSpec((2, HALF, LANES), lambda i, b: (0, 0, 0)),
            scratch_shapes=[
                pltpu.VMEM((DEPTH, sources), BF16),
                pltpu.VMEM((8, sources), F32),
                pltpu.VMEM((16, sources), BF16),
                pltpu.VMEM((272, 256), F32),
            ],
        ),
        out_shape=jax.ShapeDtypeStruct((2, HALF, LANES), F32),
        compiler_params=pltpu.CompilerParams(vmem_limit_bytes=40 << 20),
        name="moment_pass",
    )(blocks, sigma2, outlier_weight, core, all_sums, targets, kernel, panel, anchors)

    part = share[0] + lax.ppermute(share[1], "c", [(0, 1), (1, 0)])
    part = jnp.sum(lax.all_gather(part, "y"), axis=0)
    part = jnp.sum(lax.all_gather(part, "z"), axis=0)
    warp = jnp.sum(lax.all_gather(part[:WARP_ROWS], "x"), axis=0)
    both = lax.all_gather(jnp.concatenate([warp, part[WARP_ROWS:]], axis=0), "c")

    first, second = both[0], both[1]
    upper = jnp.concatenate([first[128:192], second[0:64]], axis=0)
    gram = jnp.concatenate(
        [
            jnp.concatenate([first[0:128], upper], axis=1),
            jnp.concatenate([upper.T, second[64:192]], axis=1),
        ],
        axis=0,
    )
    pulled = jnp.concatenate([first[192:195], second[192:195]], axis=1)
    total = first[195, 0]
    masses_all = both[:, WARP_ROWS:].reshape(pieces, LANES)
    place = (lax.axis_index("c") * zs + lax.axis_index("z")) * ys + lax.axis_index("y")
    masses = lax.dynamic_slice_in_dim(masses_all, place, 1, 0)[0]

    src_xyz = src_coords.astype(F32)
    basis = jnp.exp(-squared_gap(src_xyz, anchors) * (0.5 / ANCHOR_WIDTH))
    shift = warp_solve(basis, gram, pulled, total, anchors, sigma2, warp_lambda)
    return (src_xyz + shift, masses)


def solution(mesh):
    fine = Mesh(mesh.devices.reshape(8, 4, 2, 4), ("z", "y", "c", "x"))
    tgt = ("z", "y", "c")
    both = ("z", "y", "c", "x")
    placed = (
        P(None, tgt), P(None, tgt), P(tgt), P(), P(None, both), P(None, both), P(), P(), P(), P(),
    )
    return jax.shard_map(
        local, mesh=fine, in_specs=placed, out_specs=(P(None, both), P(both)), check_vma=False
    )
```

time: 928 us -> 268 us (0.29)
  matrix products: 354 us -> 2.51 us
  waiting for transfers between devices: 336 us -> 17.8 us
  Pallas kernels: 0 us -> 56.5 us
  blocking collectives: 141 us -> 108 us
    dot_general x50 -> x0, matrix products: 351 us -> none  [the longest x32 231 us: affinity(): lax.dot_general(src_feat, tgt_feat, (((0,), (0,)), ((), ())), preferred_e...]
    psum x1 -> x0, waiting for transfers between devices: 174 us -> none  [local(): gram, pulled, total = lax.psum((gram, pulled, total), ('tgt', 'src'))]
    unnamed x4 -> x1, waiting for transfers between devices: 140 us -> 0.02 us
    psum x2 -> x0, blocking collectives: 92.8 us -> none  [the longest x1 79.8 us: local(): gram, pulled, total = lax.psum((gram, pulled, total), ('tgt', 'src'))]
    all_gather x1 -> x7, blocking collectives: 48.4 us -> 108 us  [the longest x3 44.6 us: gather(): return lax.all_gather(value, axis, axis=0, tiled=True)]
    pallas_call x0 -> x3, Pallas kernels: none -> 56.5 us  [the longest x1 28.8 us: local(): pl.pallas_call(functools.partial(moment_pass, total_sources=sources * xs)...]
  transfers between devices with their start and end apart: 3 -> 2, of which waited for: 3 -> 2; matrix products, arithmetic and copies ran while one was open for 1% -> 1% of each run, Pallas kernels for 0% -> 1%
where the time goes in v1:
time: 268 us; the launch traced here: 269 us
  blocking collectives  108 us (40%)
  other arithmetic  56.9 us (21%)
  Pallas kernels  56.5 us (21%)
  waiting for transfers between devices  17.8 us (7%)
  between operations  17.4 us (6%)
  local copies, waits for them, and re-layouts  9.14 us (3%)
    all_gather x3, blocking collectives, gather(): return lax.all_gather(value, axis, axis=0, tiled=True)  44.6 us
    another operation x6, other arithmetic, warp_solve(): factor = jnp.linalg.cholesky(system)  34 us
    all_gather x1, blocking collectives, local(): part = jnp.sum(lax.all_gather(part, 'z'), axis=0)  31.4 us
    pallas_call x1, Pallas kernels, local(): pl.pallas_call(functools.partial(moment_pass, total_sources=sources * xs)...  28.8 us
    pallas_call x1, Pallas kernels, local(): pl.pallas_call(kernel_pass, grid_spec=pltpu.PrefetchScalarGridSpec(num_sc...  24.6 us
    another operation x3, other arithmetic, warp_solve(): coeffs = jax.scipy.linalg.cho_solve((factor, True), (pulled / total).T)  19.7 us
    all_gather x1, waiting for transfers between devices, gather(): return lax.all_gather(value, axis, axis=0, tiled=True)  17.2 us
    all_gather x1, blocking collectives, local(): lax.all_gather(jnp.concatenate([warp, part[WARP_ROWS:]], axis=0), 'c')  11.5 us
  transfers between devices with their start and end apart: 2, of which 2 were waited for; matrix products, arithmetic and copies ran while one was open for 1% of the time, Pallas kernels for 1%

profile of v1, /device:TPU:1, one launch (start us, length us, event | category | flops | bytes accessed | tf_op | source)
XLA Modules:
  0.0 268.8 jit_solution(2439964788892037278)
XLA Ops:
  7.2 0.0 all-gather.8.cloned.1.call-start
  7.2 0.1 pad.19.clone
  7.3 0.8 maximum_maximum_fusion.1
  8.1 10.4 %all-gather = bf16[320,128]{1,0:T(8,128)(2,1)S(1)} all-gather(bf16[80,128]{1,0:T(8,128)(2,1)S(1)} %maximum_maximum_fusion.1), channel_id=2, replica_groups=mesh['z'=8,'y'=4,'c'=2,'x'=4] {'y'}, dimensions={0}, use_global_device_ids=true | all-gather | bytes 102400 | tf_op jit(solution)/shard_map/all_gather | solution.py:257
  18.5 25.2 %all_gather.37 = bf16[32,80,128]{2,1,0:T(8,128)(2,1)} all-gather(bf16[4,80,128]{2,1,0:T(8,128)(2,1)S(1)} %bitcast.86), channel_id=1, replica_groups=mesh['z'=8,'y'=4,'c'=2,'x'=4] {'z'}, dimensions={0}, use_global_device_ids=true | all-gather | bytes 737280 | tf_op jit(solution)/shard_map/all_gather | solution.py:257
  43.7 0.0 all-gather.8.cloned.1.call-update
  43.8 0.7 convert_element_type.6
  45.8 3.2 %prepare_targets.1 = (bf16[4608,256]{1,0:T(8,128)(2,1)}, s32[1]{0:T(128)}) custom-call(s32[8]{0:T(128)} %perm_ref.1, s32[512]{0:T(512)} %count_ref.1, f32[1]{0:T(128)S(6)} %copy.33.sigma2_ref, bf16[3,4096]{1,0:T(4,128)(2,1)} %xyz_ref.1, bf16[64,4096]{1,0:T(8,128)(2,1)} %feat_ref.1), custom_call_target="tpu_custom_call" | custom-call | tf_op jit(solution)/shard_map/prepare_targets/pallas_call | solution.py:273
  48.9 0.8 fusion.38
  49.7 17.2 %all-gather.8.cloned.1.call-done.panel_ref = bf16[64,80,128]{2,1,0:T(8,128)(2,1)} async-done(((bf16[32,80,128]{2,1,0:T(8,128)(2,1)}), bf16[64,80,128]{2,1,0:T(8,128)(2,1)}) %all-gather.8.cloned.1.call-update) | async-done | bytes 1310736 | tf_op jit(solution)/shard_map/all_gather | solution.py:257
  66.9 1.7 copy-done
  68.6 1.3 copy-done.1
  69.9 24.6 %kernel_pass.1 = (bf16[3584,8192]{1,0:T(8,128)(2,1)}, f32[16,256]{1,0:T(8,128)S(1)}) custom-call(s32[1]{0:T(128)} %get-tuple-element.6.blocks_ref, f32[1]{0:T(128)S(6)} %copy.33.sigma2_ref, bf16[4608,256]{1,0:T(8,128)(2,1)S(1)} %copy-done, bf16[64,80,128]{2,1,0:T(8,128)(2,1)S(1)} %copy-done.1), custom_call_target="tpu_custom_call" | custom-call | tf_op jit(solution)/shard_map/kernel_pass/pallas_call | solution.py:290
  94.5 9.0 %all-gather.1 = f32[64,256]{1,0:T(8,128)S(1)} all-gather(f32[16,256]{1,0:T(8,128)S(1)} %get-tuple-element.8), channel_id=3, replica_groups=mesh['z'=8,'y'=4,'c'=2,'x'=4] {'x'}, dimensions={0}, use_global_device_ids=true | all-gather | bytes 81920 | tf_op jit(solution)/shard_map/all_gather | solution.py:257
  103.5 28.8 %moment_pass.1 = f32[2,232,128]{2,1,0:T(8,128)S(1)} custom-call(s32[1]{0:T(128)} %get-tuple-element.6.blocks_ref, f32[1]{0:T(128)S(6)} %copy.33.sigma2_ref, f32[1]{0:T(128)S(6)} %copy.34.outlier_ref, s32[1]{0:T(128)} %bitcast.core_ref, f32[4,16,256]{2,1,0:T(8,128)S(1)} %bitcast.78, bf16[4608,256]{1,0:T(8,128)(2,1)S(1)} %copy-done, ...), custom_call_target="tpu_custom_call" | custom-call | tf_op jit(solution)/shard_map/moment_pass/pallas_call | solution.py:317
  132.3 0.1 collective-permute-start
  133.1 0.6 collective-permute-done
  133.7 10.7 %all-gather.2 = f32[928,128]{1,0:T(8,128)S(1)} all-gather(f32[232,128]{1,0:T(8,128)S(1)} %fusion.13), channel_id=4, replica_groups=mesh['z'=8,'y'=4,'c'=2,'x'=4] {'y'}, dimensions={0}, use_global_device_ids=true | all-gather | bytes 593920 | tf_op jit(solution)/shard_map/all_gather | solution.py:346
  144.5 31.4 %all-gather.3 = f32[1856,128]{1,0:T(8,128)S(1)} all-gather(f32[232,128]{1,0:T(8,128)S(1)} %reduce_sum.27), channel_id=5, replica_groups=mesh['z'=8,'y'=4,'c'=2,'x'=4] {'z'}, dimensions={0}, use_global_device_ids=true | all-gather | bytes 1069056 | tf_op jit(solution)/shard_map/all_gather | solution.py:347
  175.9 9.9 %all-gather.4 = f32[800,128]{1,0:T(8,128)S(1)} all-gather(f32[200,128]{1,0:T(8,128)S(1)} %slice.190), channel_id=6, replica_groups=mesh['z'=8,'y'=4,'c'=2,'x'=4] {'x'}, dimensions={0}, use_global_device_ids=true | all-gather | bytes 512000 | tf_op jit(solution)/shard_map/all_gather | solution.py:348
  185.9 11.5 %all-gather.5 = f32[464,128]{1,0:T(8,128)S(1)} all-gather(f32[232,128]{1,0:T(8,128)S(1)} %pad_maximum_fusion), channel_id=7, replica_groups=mesh['z'=8,'y'=4,'c'=2,'x'=4] {'c'}, dimensions={0}, use_global_device_ids=true | all-gather | bytes 356352 | tf_op jit(solution)/shard_map/all_gather | solution.py:349
  197.4 0.5 slice.196
  197.9 0.1 copy.21
  198.0 0.1 copy.23
  198.1 0.9 fusion
  199.0 0.1 copy.22
  199.2 11.7 %cholesky.50 = f32[128,128]{1,0:T(8,128)S(1)} custom-call(f32[128,128]{1,0:T(8,128)S(1)} %cholesky.118), custom_call_target="Cholesky" | custom-call | tf_op jit(solution)/shard_map/jit(cholesky)/cholesky | solution.py:248
  211.0 9.8 %custom-call.18 = f32[1,128,128]{1,2,0:T(8,128)S(1)} custom-call(f32[1,128,128]{2,1,0:T(8,128)S(1)} %get-tuple-element.37), custom_call_target="InvertDiagBlocksLowerTriangular" | custom-call | tf_op jit(solution)/shard_map/jit(cholesky)/cholesky | solution.py:248
  220.8 0.2 constant_dynamic-update-slice_fusion
  221.0 0.3 convolution_subtract_fusion
  221.3 11.7 %cholesky.105 = f32[128,128]{1,0:T(8,128)S(1)} custom-call(f32[128,128]{1,0:T(8,128)S(1)} %convolution_subtract_fusion), custom_call_target="Cholesky" | custom-call | tf_op jit(solution)/shard_map/jit(cholesky)/cholesky | solution.py:248
  233.0 0.7 compare_reduce_fusion
  234.9 0.1 triangular_solve.69
  235.0 4.0 %while.1 = (s32[]{:T(128)}, f32[256,256]{1,0:T(8,128)S(1)}, s32[2,2]{1,0:T(2,128)S(1)}, f32[2,128,128]{2,1,0:T(8,128)S(1)}, s32[]{:T(128)}) while((s32[]{:T(128)}, f32[256,256]{1,0:T(8,128)S(1)}, s32[2,2]{1,0:T(2,128)S(1)}, f32[2,128,128]{2,1,0:T(8,128)S(1)}, s32[]{:T(128)}) %tuple.34), condition=%wide.while_cond, body=%wide.while_body.sunk | while | flops 2 | bytes 131181 | solution.py:249
  235.2 0.6 fusion.47
  235.8 1.3 bitcast_dynamic-update-slice_fusion.2
  237.1 0.6 fusion.47
  237.7 1.3 bitcast_dynamic-update-slice_fusion.2
  239.0 19.7 %custom-call.19 = f32[2,128,128]{1,2,0:T(8,128)S(1)} custom-call(f32[2,128,128]{2,1,0:T(8,128)S(1)} %get-tuple-element.17), custom_call_target="InvertDiagBlocksLowerTriangular" | custom-call | tf_op jit(solution)/shard_map/jit(_cho_solve)/triangular_solve | solution.py:249
  258.6 0.7 fusion.30
  259.3 0.2 fusion.25
  259.5 0.2 convolution_subtract_fusion.2
  259.6 0.2 fusion.27
  259.8 0.2 fusion.26
  260.0 0.2 convolution_subtract_fusion.1
  260.2 0.2 fusion.24
  260.4 0.6 dynamic-slice_bitcast_fusion
  261.0 0.9 convolution_add_fusion
  (32 shorter events, 0.4 us)
Async XLA Ops:
  7.2 59.8 %all-gather.8.cloned.1.call-start = ((), (), s32[]{:S(2)}) async-start(), calls=%async_computation | async-start | bytes 1966080 | tf_op jit(solution)/shard_map/all_gather | solution.py:257
  43.7 59.8 %copy-start.2 = (f32[3,256]{1,0:T(4,128)S(1)}, f32[3,256]{1,0:T(4,128)}, u32[]{:S(2)}) copy-start(f32[3,256]{1,0:T(4,128)} %anchors_ref.1) | copy-start | bytes 9220
  66.9 1.7 copy-start
  68.6 1.3 copy-start.1
  132.3 1.4 collective-permute-start
  199.0 62.0 %copy-start.3 = (bf16[3,128]{1,0:T(4,128)(2,1)S(1)}, bf16[3,128]{1,0:T(4,128)(2,1)}, u32[]{:S(2)}) copy-start(bf16[3,128]{1,0:T(4,128)(2,1)} %param.14) | copy-start | bytes 2308
Sparse Core Ops, SparseCore 0:
  43.9 22.9 all-gather.7

commit v2 on v1

v2 whole, which is shorter than its diff:
```python
import functools
import math

import jax
import jax.numpy as jnp
from jax import lax
from jax.experimental import pallas as pl
from jax.experimental.pallas import tpu as pltpu
from jax.sharding import Mesh
from jax.sharding import PartitionSpec as P

TILE = 512
SCORE_GAIN = 4.0
ANCHOR_WIDTH = 0.1
LOG2E = math.log2(math.e)

ROWS = 256
LANES = 128
DEPTH = 256
STORED = 14
MASKED = -30000.0
GRAM_ROWS = 6

F32 = jnp.float32
BF16 = jnp.bfloat16
WHOLE = pl.BlockSpec(memory_space=pltpu.VMEM)
SCALAR = pl.BlockSpec(memory_space=pltpu.SMEM)


def split3(value):
    high = value.astype(BF16).astype(F32)
    rest = value - high
    middle = rest.astype(BF16).astype(F32)
    return high, middle, rest - middle


def pick_rows(rows, count):
    width = rows[0].shape[1]
    place = lax.broadcasted_iota(jnp.int32, (count, width), 0)
    out = jnp.zeros((count, width), F32)
    for index, row in enumerate(rows):
        out = jnp.where(place == index, row, out)
    return out


def prepare(
    perm_ref, count_ref, sigma2_ref, xyz_ref, feat_ref, src_xyz_ref, src_feat_ref,
    lots_ref, tgt_ref, blocks_ref,
):
    one = jnp.ones((1, LANES), F32)
    inv = (0.5 * LOG2E) / jnp.full((1, LANES), sigma2_ref[0], F32)
    y = src_xyz_ref[...].astype(F32)
    y = [y[c : c + 1] for c in range(3)]
    square = -(y[0] * y[0] + y[1] * y[1] + y[2] * y[2]) * inv
    side = pick_rows([*y, *y, *y, *split3(square), one, one, one], 16)
    source = jnp.concatenate([src_feat_ref[...], side.astype(BF16)], axis=0)
    for lot in range(lots_ref.shape[0]):
        lots_ref[lot] = source

    gain = SCORE_GAIN / 64 * LOG2E
    inv = (0.5 * LOG2E) / jnp.full((1, TILE), sigma2_ref[0], F32)
    one = jnp.ones((1, TILE), F32)
    lane = lax.broadcasted_iota(jnp.int32, (1, TILE), 1)
    tiles = perm_ref.shape[0]
    offset = jnp.int32(0)
    for tile in range(tiles):
        span = slice(tile * TILE, (tile + 1) * TILE)
        count = count_ref[perm_ref[tile]]
        xyz = xyz_ref[:, span].astype(F32)
        x = [xyz[c : c + 1] for c in range(3)]
        square = -(x[0] * x[0] + x[1] * x[1] + x[2] * x[2]) * inv
        parts = [split3(row * (2.0 * inv)) for row in x]
        own = split3(jnp.where(lane < count, square, MASKED))
        rows = [part[level] for level in range(3) for part in parts] + [one, one, one, *own]
        rows = rows + [jnp.zeros_like(one)] + [*x, one] * 2
        high, middle, low = split3(feat_ref[:, span].astype(F32) * gain)
        wide = jnp.concatenate(
            [high, pick_rows(rows, 24), jnp.zeros((40, TILE), F32), middle, low], axis=0
        )
        tgt_ref[pl.ds(pl.multiple_of(offset, 16), TILE), :] = wide.T.astype(BF16)
        offset = offset + ((count + 15) // 16) * 16
    blank = jnp.where(lax.broadcasted_iota(jnp.int32, (ROWS, DEPTH), 1) == 76, MASKED, 0.0)
    tgt_ref[pl.ds(pl.multiple_of(offset, 16), ROWS), :] = blank.astype(BF16)
    blocks_ref[0] = (offset + ROWS - 1) // ROWS


def widened(wide_ref, start, width):
    feat = wide_ref[0:64, start : start + width]
    return jnp.concatenate([wide_ref[:, start : start + width], feat, feat], axis=0)


def kernel_pass(blocks_ref, tgt_ref, own_ref, other_ref, kernel_ref, sum_ref, wide_ref):
    step = pl.program_id(0)

    @pl.when(step == 0)
    def _():
        wide_ref[80:128, :] = jnp.zeros((48, wide_ref.shape[1]), BF16)
        for lot, panel_ref in enumerate((own_ref, other_ref)):
            for piece in range(panel_ref.shape[0]):
                start = (lot * panel_ref.shape[0] + piece) * LANES
                wide_ref[0:80, start : start + LANES] = panel_ref[piece]

    def block(store):
        tgt = tgt_ref[...]
        total = jnp.zeros((ROWS, LANES), F32)
        for start in range(0, wide_ref.shape[1], 256):
            score = jnp.dot(tgt, widened(wide_ref, start, 256), preferred_element_type=F32)
            value = jnp.exp2(score)
            rounded = value.astype(BF16)
            if store:
                kernel_ref[:, start : start + 256] = rounded
            value = rounded.astype(F32)
            total += value[:, 0:128] + value[:, 128:256]
        sum_ref[pl.ds(step, 1), :] = jnp.sum(total.T, axis=0, keepdims=True)

    blocks = blocks_ref[0]

    @pl.when((step < STORED) & (step < blocks))
    def _():
        block(True)

    @pl.when((step >= STORED) & (step < blocks))
    def _():
        block(False)


def warp_sums(acc_ref, side_ref, anchors_ref, core_ref, out_ref, gram_ref):
    pieces = out_ref.shape[1]
    sources = side_ref.shape[1]
    count = anchors_ref.shape[1]
    rate = 0.5 / ANCHOR_WIDTH * LOG2E
    a0, a1, a2 = anchors_ref[0:1, :], anchors_ref[1:2, :], anchors_ref[2:3, :]
    square = -(a0 * a0 + a1 * a1 + a2 * a2) * rate
    parts = [split3(row * (2.0 * rate)) for row in (a0, a1, a2)]
    zero = jnp.zeros((1, count), F32)
    rows = [part[level] for level in range(3) for part in parts] + [zero] * 3 + [*split3(square)]
    anchor_side = pick_rows(rows, LANES).T.astype(BF16)[:, 0:16]
    sums = acc_ref[...]
    sums = sums + pltpu.roll(sums, 4, 0)
    acc_ref[...] = sums
    gram_ref[...] = jnp.zeros_like(gram_ref)
    width = 2048

    def chunk(index, unused):
        at = pl.ds(pl.multiple_of(index * width, width), width)
        side = side_ref[:, at]
        y = side.astype(F32)[0:8]
        y0, y1, y2 = y[0:1], y[1:2], y[2:3]
        square = (y0 * y0 + y1 * y1 + y2 * y2) * rate
        basis = jnp.exp2(jnp.dot(anchor_side, side, preferred_element_type=F32) - square)
        moment = acc_ref[:, at]
        mass = moment[3:4, :]
        pull = moment - mass * y
        left = jnp.concatenate([basis * mass, pull, jnp.zeros_like(pull)], axis=0)
        left_high = left.astype(BF16)
        left_low = (left - left_high.astype(F32)).astype(BF16)
        basis_high = basis.astype(BF16)
        basis_low = (basis - basis_high.astype(F32)).astype(BF16)
        last = (((1,), (1,)), ((), ()))
        first = lax.dot_general(
            jnp.concatenate([left_high, left_low], axis=0), basis_high, last, preferred_element_type=F32
        )
        second = lax.dot_general(left_high, basis_low, last, preferred_element_type=F32)
        gram_ref[...] += first[0:272] + first[272:544] + second
        return unused

    lax.fori_loop(0, sources // width, chunk, 0)
    total = jnp.sum(acc_ref[3:4, :])
    row = lax.broadcasted_iota(jnp.int32, (8, LANES), 0)
    core = core_ref[0]
    out_ref[:, :, GRAM_ROWS : GRAM_ROWS + 1, :] = jnp.zeros((2, pieces, 1, LANES), F32)
    for half in range(2):
        at = jnp.where(core == half, 0, 1)
        for piece in range(pieces):
            start = piece * GRAM_ROWS
            for r in range(start, start + GRAM_ROWS):
                if half == 0:
                    line = gram_ref[r : r + 1, 0:128] if r < 128 else gram_ref[r - 128 : r - 127, 128:256]
                else:
                    line = gram_ref[r + 64 : r + 65, 128:256]
                out_ref[at, piece, r - start : r - start + 1, :] = line
            s = (half * pieces + piece) * LANES
            out_ref[half, piece, 7:8, :] = acc_ref[3:4, s : s + LANES]
        pulled = gram_ref[256:264, half * LANES : (half + 1) * LANES]
        pulled = jnp.where(row == 3, total, pulled)
        for r in range(4):
            out_ref[at, r, GRAM_ROWS : GRAM_ROWS + 1, :] = pulled[r : r + 1]


def moment_pass(
    blocks_ref, outlier_ref, core_ref, sum0_ref, sum1_ref, sum2_ref, sum3_ref, tgt_ref,
    kernel_ref, side_ref, wide_hbm_ref, anchors_ref, out_ref, wide_ref, acc_ref, gram_ref, arrived, *,
    total_sources,
):
    step = pl.program_id(0)

    @pl.when(step == 0)
    def _():
        acc_ref[...] = jnp.zeros_like(acc_ref)

    outlier = jnp.full((1, ROWS), outlier_ref[0], F32)
    floor = outlier / (1.0 - outlier) * total_sources
    normal = floor
    for ref in (sum0_ref, sum1_ref, sum2_ref, sum3_ref):
        normal = normal + ref[pl.ds(step, 1), :]
    side = tgt_ref[:, 0:128].astype(F32).T[80:88]
    weight = side / normal
    high = weight.astype(BF16).astype(F32)
    row = lax.broadcasted_iota(jnp.int32, weight.shape, 0)
    weight = jnp.where(row < 4, high, weight - high).astype(BF16)

    blocks = blocks_ref[0]

    @pl.when((step < STORED) & (step < blocks))
    def _():
        for start in range(0, kernel_ref.shape[1], 1024):
            at = slice(start, start + 1024)
            acc_ref[:, at] += jnp.dot(weight, kernel_ref[:, at], preferred_element_type=F32)

    @pl.when((step == STORED) & (step < blocks))
    def _():
        copy = pltpu.make_async_copy(wide_hbm_ref, wide_ref, arrived)
        copy.start()
        copy.wait()

    @pl.when((step >= STORED) & (step < blocks))
    def _():
        for start in range(0, wide_ref.shape[1], 512):
            at = slice(start, start + 512)
            score = jnp.dot(tgt_ref[...], widened(wide_ref, start, 512), preferred_element_type=F32)
            value = jnp.exp2(score).astype(BF16)
            acc_ref[:, at] += jnp.dot(weight, value, preferred_element_type=F32)

    @pl.when(step == blocks - 1)
    def _():
        warp_sums(acc_ref, side_ref, anchors_ref, core_ref, out_ref, gram_ref)


def squared_gap(first, second):
    gap_a, gap_b, gap_c = (first[c] - second[c] for c in range(3))
    return gap_a * gap_a + gap_b * gap_b + gap_c * gap_c


def halves(value):
    high = value.astype(BF16)
    return high, (value - high.astype(F32)).astype(BF16)


def dot3(first, second):
    (a, b), (c, d) = first, second
    wide = functools.partial(jnp.dot, preferred_element_type=F32)
    return wide(a, c) + (wide(a, d) + wide(b, c))


def dot_full(first, second):
    return jnp.dot(first, second, precision=lax.Precision.HIGHEST, preferred_element_type=F32)


def warp_update(
    sigma2_ref, lambda_ref, anchors_ref, xyz_ref, mass_ref, sums_ref, out_ref, out_mass_ref,
    system_ref, inverse_ref,
):
    pieces = sums_ref.shape[1]
    count = anchors_ref.shape[1]
    for half in range(2):
        for piece in range(pieces):
            for r in range(piece * GRAM_ROWS, (piece + 1) * GRAM_ROWS):
                line = sums_ref[half, piece, r - piece * GRAM_ROWS : r - piece * GRAM_ROWS + 1, :]
                if half == 1:
                    system_ref[r + 64 : r + 65, 128:256] = line
                elif r < 128:
                    system_ref[r : r + 1, 0:128] = line
                else:
                    system_ref[r - 128 : r - 127, 128:256] = line
    system_ref[128:256, 0:128] = system_ref[0:128, 128:256].T
    pulled = [
        jnp.concatenate([sums_ref[half, r, GRAM_ROWS : GRAM_ROWS + 1, :] for half in range(2)], axis=1)
        for r in range(3)
    ]
    total = sums_ref[0, 3, GRAM_ROWS : GRAM_ROWS + 1, 0:1]
    pulled = pick_rows(pulled, 8) / total

    rows = [anchors_ref[c : c + 1, :] for c in range(3)]
    columns = jnp.concatenate([pick_rows(rows, 8), jnp.zeros((120, count), F32)], axis=0).T
    columns = [columns[:, c : c + 1] for c in range(3)]
    rate = 0.5 / ANCHOR_WIDTH
    anchor_gram = jnp.exp(-squared_gap(columns, rows) * rate)
    place = lax.broadcasted_iota(jnp.int32, (count, count), 0)
    eye = jnp.where(place == lax.broadcasted_iota(jnp.int32, (count, count), 1), 1.0, 0.0)
    weight = lambda_ref[0] * sigma2_ref[0]
    system = system_ref[...] / total + weight * (anchor_gram + eye)
    system_ref[...] = system

    low = weight
    high = jnp.max(jnp.sum(jnp.abs(system), axis=0, keepdims=True)) * 1.0001
    start = 2.0 / jnp.full((1, count), low + high, F32)
    bound = jnp.max(jnp.full((8, LANES), high - low, F32) / jnp.full((8, LANES), high + low, F32))

    def narrowed(bound):
        square = jnp.full((8, LANES), bound * bound, F32)
        return jnp.max(2.0 / (2.0 - square)), jnp.max(square / (2.0 - square))

    scale, bound = narrowed(bound)
    inverse_ref[...] = (scale * start) * (2.0 * eye - start * system)
    system_halves = halves(system)

    def improve(bound):
        scale, after = narrowed(bound)
        inverse = inverse_ref[...]
        parts = halves(inverse)
        residual = 2.0 * eye - dot3(system_halves, parts)
        inverse_ref[...] = scale * dot3(parts, halves(residual))
        return after

    lax.while_loop(lambda bound: bound > 1e-4, improve, bound)
    inverse = inverse_ref[...]
    coeffs = dot_full(pulled, inverse)
    for _ in range(3):
        coeffs = coeffs + dot_full(pulled - dot_full(coeffs, system), inverse)

    xyz = xyz_ref[...].astype(F32)
    basis = jnp.exp(-squared_gap(columns, [xyz[c : c + 1] for c in range(3)]) * rate)
    out_ref[...] = xyz + dot_full(coeffs, basis)[0:3]
    out_mass_ref[...] = mass_ref[7:8, :]


def spread(value, axes):
    lots = jnp.broadcast_to(value, (lax.axis_size(axes), *value.shape[1:]))
    return lax.all_to_all(lots, axes, 0, 0, tiled=True)


def turned(value, axis, by):
    size = lax.axis_size(axis)
    return lax.ppermute(value, axis, [(i, (i + by) % size) for i in range(size)])


def local(
    tgt_coords, tgt_embed, tile_perm, tile_count, src_coords, src_embed, anchors, sigma2,
    outlier_weight, warp_lambda,
):
    cells = tgt_coords.shape[1]
    zs, ys, cs, xs = (lax.axis_size(name) for name in ("z", "y", "c", "x"))
    pieces = zs * ys
    sources = pieces * cs * LANES
    blocks_max = cells // ROWS

    lots, targets, blocks = pl.pallas_call(
        prepare,
        in_specs=[SCALAR, SCALAR, SCALAR, WHOLE, WHOLE, WHOLE, WHOLE],
        out_specs=[WHOLE, WHOLE, SCALAR],
        out_shape=[
            jax.ShapeDtypeStruct((pieces, 80, LANES), BF16),
            jax.ShapeDtypeStruct((cells + TILE, DEPTH), BF16),
            jax.ShapeDtypeStruct((1,), jnp.int32),
        ],
        name="prepare",
    )(tile_perm, tile_count, sigma2, tgt_coords, tgt_embed, src_coords, src_embed)

    own = lax.all_to_all(lots, ("z", "y"), 0, 0, tiled=True)
    other = lax.ppermute(own, "c", [(0, 1), (1, 0)])

    def at_block(i, b):
        return jnp.minimum(i, b[0] - 1), 0

    def at_stored(i, b):
        return jnp.minimum(jnp.minimum(i, b[0] - 1), STORED - 1), 0

    kernel, sums, wide = pl.pallas_call(
        kernel_pass,
        grid_spec=pltpu.PrefetchScalarGridSpec(
            num_scalar_prefetch=1,
            grid=(blocks_max,),
            in_specs=[
                pl.BlockSpec((ROWS, DEPTH), at_block),
                pl.BlockSpec((pieces, 80, LANES), lambda i, b: (0, 0, 0)),
                pl.BlockSpec((pieces, 80, LANES), lambda i, b: (0, 0, 0)),
            ],
            out_specs=[
                pl.BlockSpec((ROWS, sources), at_stored),
                pl.BlockSpec((blocks_max, ROWS), lambda i, b: (0, 0)),
                pl.BlockSpec((DEPTH // 2, sources), lambda i, b: (0, 0)),
            ],
        ),
        out_shape=[
            jax.ShapeDtypeStruct((STORED * ROWS, sources), BF16),
            jax.ShapeDtypeStruct((blocks_max, ROWS), F32),
            jax.ShapeDtypeStruct((DEPTH // 2, sources), BF16),
        ],
        compiler_params=pltpu.CompilerParams(vmem_limit_bytes=40 << 20),
        name="kernel_pass",
    )(blocks, targets, own, other)

    all_sums = [sums] + [turned(sums, "x", by) for by in range(1, xs)]

    core = lax.axis_index("c").astype(jnp.int32)[None]
    share = pl.pallas_call(
        functools.partial(moment_pass, total_sources=sources * xs),
        grid_spec=pltpu.PrefetchScalarGridSpec(
            num_scalar_prefetch=1,
            grid=(blocks_max,),
            in_specs=[
                SCALAR,
                SCALAR,
                *[pl.BlockSpec((blocks_max, ROWS), lambda i, b: (0, 0))] * xs,
                pl.BlockSpec((ROWS, DEPTH), at_block),
                pl.BlockSpec((ROWS, sources), at_stored),
                pl.BlockSpec((16, sources), lambda i, b: (4, 0)),
                pl.BlockSpec(memory_space=pltpu.HBM),
                pl.BlockSpec((3, 256), lambda i, b: (0, 0)),
            ],
            out_specs=pl.BlockSpec((cs, pieces, 8, LANES), lambda i, b: (0, 0, 0, 0)),
            scratch_shapes=[
                pltpu.VMEM((DEPTH // 2, sources), BF16),
                pltpu.VMEM((8, sources), F32),
                pltpu.VMEM((272, 256), F32),
                pltpu.SemaphoreType.DMA,
            ],
        ),
        out_shape=jax.ShapeDtypeStruct((cs, pieces, 8, LANES), F32),
        compiler_params=pltpu.CompilerParams(vmem_limit_bytes=40 << 20),
        name="moment_pass",
    )(blocks, outlier_weight, core, *all_sums, targets, kernel, wide, wide, anchors)

    part = share[0] + lax.ppermute(share[1], "c", [(0, 1), (1, 0)])
    part = jnp.sum(lax.all_to_all(part, ("z", "y"), 0, 0, tiled=True), axis=0)
    total = part + turned(part, "x", 1) + turned(part, "x", 2) + turned(part, "x", 3)
    both = lax.all_gather(spread(total[None], ("z", "y")), "c")

    warped, masses = pl.pallas_call(
        warp_update,
        in_specs=[SCALAR, SCALAR, WHOLE, WHOLE, WHOLE, WHOLE],
        out_specs=[WHOLE, WHOLE],
        out_shape=[jax.ShapeDtypeStruct((3, LANES), F32), jax.ShapeDtypeStruct((1, LANES), F32)],
        scratch_shapes=[pltpu.VMEM((256, 256), F32)] * 2,
        name="warp_update",
    )(sigma2, warp_lambda, anchors, src_coords, part, both)
    return (warped, masses.reshape(LANES))


def solution(mesh):
    fine = Mesh(mesh.devices.reshape(8, 4, 2, 4), ("z", "y", "c", "x"))
    tgt = ("z", "y", "c")
    both = ("z", "y", "c", "x")
    placed = (
        P(None, tgt), P(None, tgt), P(tgt), P(), P(None, both), P(None, both), P(), P(), P(), P(),
    )
    return jax.shard_map(
        local, mesh=fine, in_specs=placed, out_specs=(P(None, both), P(both)), check_vma=False
    )
```

time: 268 us -> 156 us (0.58)
  other arithmetic: 56.9 us -> 0.06 us
  blocking collectives: 108 us -> 55.2 us
  starting transfers between devices: 0.13 us -> 30.7 us
  between operations: 17.4 us -> 2.65 us
  Pallas kernels: 56.5 us -> 45.6 us
  local copies, waits for them, and re-layouts: 9.14 us -> 5.28 us
  waiting for transfers between devices: 17.8 us -> 15 us
    all_gather x7 -> x1, blocking collectives: 108 us -> 5.93 us  [local(): both = lax.all_gather(spread(total[None], ('z', 'y')), 'c')]
    another operation x9 -> x0, other arithmetic: 53.7 us -> none  [the longest x6 34 us: warp_solve(): factor = jnp.linalg.cholesky(system)]
    all_to_all x0 -> x2, blocking collectives: none -> 49.3 us  [the longest x1 30.7 us: local(): own = lax.all_to_all(lots, ('z', 'y'), 0, 0, tiled=True)]
    all_gather x1 -> x0, waiting for transfers between devices: 17.2 us -> none  [gather(): return lax.all_gather(value, axis, axis=0, tiled=True)]
    ppermute x1, starting transfers between devices: 0.09 us -> 15.9 us  [local(): part = share[0] + lax.ppermute(share[1], 'c', [(0, 1), (1, 0)])]
    ppermute x0 -> x7, starting transfers between devices: none -> 10.9 us  [the longest x6 8.47 us: turned(): lax.ppermute(value, axis, [(i, (i + by) % size) for i in range(size)])]
    pallas_call x1, Pallas kernels: 28.8 us -> 18.4 us  [local(): pl.pallas_call(functools.partial(moment_pass, total_sources=sources * xs)...]
    pallas_call x1, Pallas kernels: 24.6 us -> 15.6 us  [local(): pl.pallas_call(kernel_pass, grid_spec=pltpu.PrefetchScalarGridSpec(num_sc...]
  transfers between devices with their start and end apart: 2 -> 9, of which waited for: 2 -> 7; matrix products, arithmetic and copies ran while one was open for 1% -> 0% of each run, Pallas kernels for 1% -> 0%
where the time goes in v2:
time: 156 us; the launch traced here: 154 us
  blocking collectives  55.2 us (35%)
  Pallas kernels  45.6 us (29%)
  starting transfers between devices  30.7 us (20%)
  waiting for transfers between devices  15 us (10%)
  local copies, waits for them, and re-layouts  5.28 us (3%)
  between operations  2.65 us (2%)
    all_to_all x1, blocking collectives, local(): own = lax.all_to_all(lots, ('z', 'y'), 0, 0, tiled=True)  30.7 us
    all_to_all x1, blocking collectives, local(): part = jnp.sum(lax.all_to_all(part, ('z', 'y'), 0, 0, tiled=True), axis=0)  18.6 us
    pallas_call x1, Pallas kernels, local(): pl.pallas_call(functools.partial(moment_pass, total_sources=sources * xs)...  18.4 us
    ppermute x1, starting transfers between devices, local(): part = share[0] + lax.ppermute(share[1], 'c', [(0, 1), (1, 0)])  15.9 us
    pallas_call x1, Pallas kernels, local(): pl.pallas_call(kernel_pass, grid_spec=pltpu.PrefetchScalarGridSpec(num_sc...  15.6 us
    all_to_all x1, waiting for transfers between devices, spread(): return lax.all_to_all(lots, axes, 0, 0, tiled=True)  8.76 us
    ppermute x6, starting transfers between devices, turned(): lax.ppermute(value, axis, [(i, (i + by) % size) for i in range(size)])  8.47 us
    pallas_call x1, Pallas kernels, local(): pl.pallas_call(warp_update, in_specs=[SCALAR, SCALAR, WHOLE, WHOLE, WHOLE...  7.84 us
  transfers between devices with their start and end apart: 9, of which 7 were waited for; matrix products, arithmetic and copies ran while one was open for 0% of the time, Pallas kernels for 0%

profile of v2, /device:TPU:1, one launch (start us, length us, event | category | flops | bytes accessed | tf_op | source)
XLA Modules:
  0.0 154.4 jit_solution(15100066812520862636)
XLA Ops:
  1.3 3.7 %prepare.1 = (bf16[32,80,128]{2,1,0:T(8,128)(2,1)}, bf16[4608,256]{1,0:T(8,128)(2,1)}, s32[1]{0:T(128)}) custom-call(s32[8]{0:T(128)} %perm_ref.1, s32[512]{0:T(512)} %count_ref.1, f32[1]{0:T(128)S(6)} %copy.12.sigma2_ref, bf16[3,4096]{1,0:T(4,128)(2,1)} %xyz_ref.2, bf16[64,4096]{1,0:T(8,128)(2,1)} %feat_ref.1, bf16[3,128]{1,0:T(4,128)(2,1)} %xyz_ref.3, ...), custom_call_target="tpu_custom_call" | custom-call | tf_op jit(solution)/shard_map/prepare/pallas_call | solution.py:347
  5.0 0.0 copy-start.4
  5.0 30.7 %all_to_all.15.own_ref = bf16[32,80,128]{2,1,0:T(8,128)(2,1)S(1)} all-to-all(bf16[32,80,128]{2,1,0:T(8,128)(2,1)} %get-tuple-element.12), channel_id=1, replica_groups=mesh['z'=8,'y'=4,'c'=2,'x'=4] {'z','y'}, dimensions={0} | all-to-all | bytes 1310720 | tf_op jit(solution)/shard_map/all_to_all | solution.py:359
  35.8 2.5 %collective-permute-start = (bf16[32,80,128]{2,1,0:T(8,128)(2,1)S(1)}, bf16[32,80,128]{2,1,0:T(8,128)(2,1)S(1)}, u32[]{:S(2)}, u32[]{:S(2)}) collective-permute-start(bf16[32,80,128]{2,1,0:T(8,128)(2,1)S(1)} %all_to_all.15.own_ref), channel_id=1, source_target_pairs={{0,4},{4,0},{1,5},{5,1},{2,6},{6,2},{3,7},{7,3},{8,12},{12,8},{9,1... | collective-permute-start | bytes 1966088 | tf_op jit(solution)/shard_map/ppermute | solution.py:360
  38.2 1.7 %collective-permute-done.other_ref = bf16[32,80,128]{2,1,0:T(8,128)(2,1)S(1)} collective-permute-done((bf16[32,80,128]{2,1,0:T(8,128)(2,1)S(1)}, bf16[32,80,128]{2,1,0:T(8,128)(2,1)S(1)}, u32[]{:S(2)}, u32[]{:S(2)}) %collective-permute-start) | collective-permute-done | bytes 655392 | tf_op jit(solution)/shard_map/ppermute | solution.py:360
  40.0 0.0 copy-start
  40.0 1.7 %copy-done = bf16[4608,256]{1,0:T(8,128)(2,1)S(1)} copy-done((bf16[4608,256]{1,0:T(8,128)(2,1)S(1)}, bf16[4608,256]{1,0:T(8,128)(2,1)}, u32[]{:S(2)}) %copy-start) | copy-done | bytes 2359320
  41.6 0.0 copy-start.1
  41.6 15.6 %kernel_pass.1 = (bf16[3584,8192]{1,0:T(8,128)(2,1)}, f32[16,256]{1,0:T(8,128)S(1)}, bf16[128,8192]{1,0:T(8,128)(2,1)S(1)}) custom-call(s32[1]{0:T(128)} %get-tuple-element.10.blocks_ref, bf16[4608,256]{1,0:T(8,128)(2,1)S(1)} %copy-done, bf16[32,80,128]{2,1,0:T(8,128)(2,1)S(1)} %all_to_all.15.own_ref, bf16[32,80,128]{2,1,0:T(8,128)(2,1)S(1)} %collective-permute-done.other_ref), custom_call_target="tpu_custom_call" | custom-call | tf_op jit(solution)/shard_map/kernel_pass/pallas_call | solution.py:368
  57.2 0.0 copy-start.2
  57.2 1.3 copy-done.2
  58.5 1.2 collective-permute-start.1
  59.7 2.5 %collective-permute-start.2 = (f32[16,256]{1,0:T(8,128)S(1)}, f32[16,256]{1,0:T(8,128)S(1)}, u32[]{:S(2)}, u32[]{:S(2)}) collective-permute-start(f32[16,256]{1,0:T(8,128)S(1)} %get-tuple-element.13.sum0_ref), channel_id=1, source_target_pairs={{0,2},{1,3},{2,0},{3,1},{4,6},{5,7},{6,4},{7,5},{8,10},{9,11},{10,... | collective-permute-start | bytes 49160 | tf_op jit(solution)/shard_map/ppermute | solution.py:334
  62.2 1.1 collective-permute-start.3
  64.0 0.0 collective-permute-done.1.sum1_ref
  64.0 0.0 collective-permute-done.2.sum2_ref
  64.0 0.8 collective-permute-done.3.sum3_ref
  64.8 0.0 copy-done.4
  64.8 0.0 copy-done.1
  64.8 0.0 copy-start.3
  64.8 1.6 %copy-done.3 = bf16[128,8192]{1,0:T(8,128)(2,1)S(1)} copy-done((bf16[128,8192]{1,0:T(8,128)(2,1)S(1)}, bf16[128,8192]{1,0:T(8,128)(2,1)}, u32[]{:S(2)}) %copy-start.3) | copy-done | bytes 2097176
  66.4 18.4 %moment_pass.1 = f32[2,32,8,128]{3,2,1,0:T(8,128)S(1)} custom-call(s32[1]{0:T(128)} %get-tuple-element.10.blocks_ref, f32[1]{0:T(128)S(6)} %copy.13.outlier_ref, s32[1]{0:T(128)} %bitcast.core_ref, f32[16,256]{1,0:T(8,128)S(1)} %get-tuple-element.13.sum0_ref, f32[16,256]{1,0:T(8,128)S(1)} %collective-permute-done.1.sum1_ref, ...), custom_call_target="tpu_custom_call" | custom-call | tf_op jit(solution)/shard_map/moment_pass/pallas_call | solution.py:396
  84.9 15.9 %collective-permute-start.4 = (f32[32,8,128]{2,1,0:T(8,128)S(1)}, f32[32,8,128]{2,1,0:T(8,128)S(1)}, u32[]{:S(2)}, u32[]{:S(2)}) collective-permute-start(f32[32,8,128]{2,1,0:T(8,128)S(1)} %slice_bitcast_fusion), channel_id=1, source_target_pairs={{0,4},{4,0},{1,5},{5,1},{2,6},{6,2},{3,7},{7,3},{8,12},{12,8},{9,1... | collective-permute-start | bytes 393224 | tf_op jit(solution)/shard_map/ppermute | solution.py:424
  100.7 1.0 collective-permute-done.4
  101.7 18.6 %all_to_all.16 = f32[32,8,128]{2,1,0:T(8,128)S(1)} all-to-all(f32[32,8,128]{2,1,0:T(8,128)S(1)} %fusion), channel_id=1, replica_groups=mesh['z'=8,'y'=4,'c'=2,'x'=4] {'z','y'}, dimensions={0} | all-to-all | bytes 262144 | tf_op jit(solution)/shard_map/all_to_all | solution.py:425
  120.3 0.0 copy-start.5
  120.3 0.4 collective-permute-start.5
  120.7 3.3 %collective-permute-start.6 = (f32[8,128]{1,0:T(8,128)S(1)}, f32[8,128]{1,0:T(8,128)S(1)}, u32[]{:S(2)}, u32[]{:S(2)}) collective-permute-start(f32[8,128]{1,0:T(8,128)S(1)} %reduce_sum.9.mass_ref), channel_id=1, source_target_pairs={{0,2},{1,3},{2,0},{3,1},{4,6},{5,7},{6,4},{7,5},{8,10},{9,11},{10,... | collective-permute-start | bytes 12296 | tf_op jit(solution)/shard_map/ppermute | solution.py:334
  124.0 0.0 collective-permute-start.7
  124.0 0.1 collective-permute-done.5
  124.1 0.9 collective-permute-done.6
  125.0 1.7 %collective-permute-done.7 = f32[8,128]{1,0:T(8,128)S(1)} collective-permute-done((f32[8,128]{1,0:T(8,128)S(1)}, f32[8,128]{1,0:T(8,128)S(1)}, u32[]{:S(2)}, u32[]{:S(2)}) %collective-permute-start.7) | collective-permute-done | bytes 4128 | tf_op jit(solution)/shard_map/ppermute | solution.py:334
  126.7 0.7 broadcast_in_dim.10
  127.4 3.9 %all-to-all-start.2 = ((f32[32,8,128]{2,1,0:T(8,128)}), f32[32,8,128]{2,1,0:T(8,128)S(1)}, u32[]{:S(2)}, u32[]{:S(2)}) async-start(f32[32,8,128]{2,1,0:T(8,128)} %broadcast_in_dim.10), calls=%async_computation.2 | async-start | bytes 262144 | tf_op jit(solution)/shard_map/all_to_all | solution.py:329
  131.9 8.8 %all-to-all-done.2 = f32[32,8,128]{2,1,0:T(8,128)S(1)} async-done(((f32[32,8,128]{2,1,0:T(8,128)}), f32[32,8,128]{2,1,0:T(8,128)S(1)}, u32[]{:S(2)}, u32[]{:S(2)}) %all-to-all-start.2) | async-done | bytes 131104 | tf_op jit(solution)/shard_map/all_to_all | solution.py:329
  140.7 5.9 %all-gather = f32[64,8,128]{2,1,0:T(8,128)} all-gather(f32[32,8,128]{2,1,0:T(8,128)S(1)} %all-to-all-done.2), channel_id=2, replica_groups=mesh['z'=8,'y'=4,'c'=2,'x'=4] {'c'}, dimensions={0}, use_global_device_ids=true | all-gather | bytes 393216 | tf_op jit(solution)/shard_map/all_gather | solution.py:427
  146.6 0.0 copy-done.5
  146.6 7.8 %warp_update.1 = (f32[3,128]{1,0:T(4,128)}, f32[1,128]{1,0:T(1,128)}) custom-call(f32[1]{0:T(128)S(6)} %copy.12.sigma2_ref, f32[1]{0:T(128)S(6)} %copy.14.lambda_ref, f32[3,256]{1,0:T(4,128)} %anchors_ref.3, bf16[3,128]{1,0:T(4,128)(2,1)} %xyz_ref.3, f32[8,128]{1,0:T(8,128)} %copy-done.5, f32[2,32,8,128]{3,2,1,0:T(8,128)} %bitcast.9), custom_call_target="tpu_custom_call" | custom-call | tf_op jit(solution)/shard_map/warp_update/pallas_call | solution.py:429
  (4 shorter events, 0.1 us)
Async XLA Ops:
  5.0 59.8 %copy-start.4 = (f32[3,256]{1,0:T(4,128)S(1)}, f32[3,256]{1,0:T(4,128)}, u32[]{:S(2)}) copy-start(f32[3,256]{1,0:T(4,128)} %anchors_ref.3) | copy-start | bytes 9220
  35.8 4.2 %collective-permute-start = (bf16[32,80,128]{2,1,0:T(8,128)(2,1)S(1)}, bf16[32,80,128]{2,1,0:T(8,128)(2,1)S(1)}, u32[]{:S(2)}, u32[]{:S(2)}) collective-permute-start(bf16[32,80,128]{2,1,0:T(8,128)(2,1)S(1)} %all_to_all.15.own_ref), channel_id=1, source_target_pairs={{0,4},{4,0},{1,5},{5,1},{2,6},{6,2},{3,7},{7,3},{8,12},{12,8},{9,1... | collective-permute-start | bytes 1966088 | tf_op jit(solution)/shard_map/ppermute | solution.py:360
  40.0 1.7 %copy-start = (bf16[4608,256]{1,0:T(8,128)(2,1)S(1)}, bf16[4608,256]{1,0:T(8,128)(2,1)}, u32[]{:S(2)}) copy-start(bf16[4608,256]{1,0:T(8,128)(2,1)} %get-tuple-element.11.tgt_ref) | copy-start | bytes 7077892
  41.6 23.2 %copy-start.1 = (bf16[4608,256]{1,0:T(8,128)(2,1)S(1)}, bf16[4608,256]{1,0:T(8,128)(2,1)}, u32[]{:S(2)}) copy-start(bf16[4608,256]{1,0:T(8,128)(2,1)} %get-tuple-element.11.tgt_ref) | copy-start | bytes 7077892
  57.2 1.3 copy-start.2
  58.5 5.5 %collective-permute-start.1 = (f32[16,256]{1,0:T(8,128)S(1)}, f32[16,256]{1,0:T(8,128)S(1)}, u32[]{:S(2)}, u32[]{:S(2)}) collective-permute-start(f32[16,256]{1,0:T(8,128)S(1)} %get-tuple-element.13.sum0_ref), channel_id=1, source_target_pairs={{0,1},{1,2},{2,3},{3,0},{4,5},{5,6},{6,7},{7,4},{8,9},{9,10},{10,1... | collective-permute-start | bytes 49160 | tf_op jit(solution)/shard_map/ppermute | solution.py:334
  59.7 4.3 %collective-permute-start.2 = (f32[16,256]{1,0:T(8,128)S(1)}, f32[16,256]{1,0:T(8,128)S(1)}, u32[]{:S(2)}, u32[]{:S(2)}) collective-permute-start(f32[16,256]{1,0:T(8,128)S(1)} %get-tuple-element.13.sum0_ref), channel_id=1, source_target_pairs={{0,2},{1,3},{2,0},{3,1},{4,6},{5,7},{6,4},{7,5},{8,10},{9,11},{10,... | collective-permute-start | bytes 49160 | tf_op jit(solution)/shard_map/ppermute | solution.py:334
  62.2 2.6 %collective-permute-start.3 = (f32[16,256]{1,0:T(8,128)S(1)}, f32[16,256]{1,0:T(8,128)S(1)}, u32[]{:S(2)}, u32[]{:S(2)}) collective-permute-start(f32[16,256]{1,0:T(8,128)S(1)} %get-tuple-element.13.sum0_ref), channel_id=1, source_target_pairs={{0,3},{1,0},{2,1},{3,2},{4,7},{5,4},{6,5},{7,6},{8,11},{9,8},{10,9... | collective-permute-start | bytes 49160 | tf_op jit(solution)/shard_map/ppermute | solution.py:334
  64.8 1.6 %copy-start.3 = (bf16[128,8192]{1,0:T(8,128)(2,1)S(1)}, bf16[128,8192]{1,0:T(8,128)(2,1)}, u32[]{:S(2)}) copy-start(bf16[128,8192]{1,0:T(8,128)(2,1)} %copy-done.2) | copy-start | bytes 6291460
  84.9 16.9 %collective-permute-start.4 = (f32[32,8,128]{2,1,0:T(8,128)S(1)}, f32[32,8,128]{2,1,0:T(8,128)S(1)}, u32[]{:S(2)}, u32[]{:S(2)}) collective-permute-start(f32[32,8,128]{2,1,0:T(8,128)S(1)} %slice_bitcast_fusion), channel_id=1, source_target_pairs={{0,4},{4,0},{1,5},{5,1},{2,6},{6,2},{3,7},{7,3},{8,12},{12,8},{9,1... | collective-permute-start | bytes 393224 | tf_op jit(solution)/shard_map/ppermute | solution.py:424
  120.3 26.3 %copy-start.5 = (f32[8,128]{1,0:T(8,128)}, f32[8,128]{1,0:T(8,128)S(1)}, u32[]{:S(2)}) copy-start(f32[8,128]{1,0:T(8,128)S(1)} %reduce_sum.9.mass_ref) | copy-start | bytes 12292
  120.3 3.7 %collective-permute-start.5 = (f32[8,128]{1,0:T(8,128)S(1)}, f32[8,128]{1,0:T(8,128)S(1)}, u32[]{:S(2)}, u32[]{:S(2)}) collective-permute-start(f32[8,128]{1,0:T(8,128)S(1)} %reduce_sum.9.mass_ref), channel_id=1, source_target_pairs={{0,1},{1,2},{2,3},{3,0},{4,5},{5,6},{6,7},{7,4},{8,9},{9,10},{10,1... | collective-permute-start | bytes 12296 | tf_op jit(solution)/shard_map/ppermute | solution.py:334
  120.7 4.3 %collective-permute-start.6 = (f32[8,128]{1,0:T(8,128)S(1)}, f32[8,128]{1,0:T(8,128)S(1)}, u32[]{:S(2)}, u32[]{:S(2)}) collective-permute-start(f32[8,128]{1,0:T(8,128)S(1)} %reduce_sum.9.mass_ref), channel_id=1, source_target_pairs={{0,2},{1,3},{2,0},{3,1},{4,6},{5,7},{6,4},{7,5},{8,10},{9,11},{10,... | collective-permute-start | bytes 12296 | tf_op jit(solution)/shard_map/ppermute | solution.py:334
  124.0 2.8 %collective-permute-start.7 = (f32[8,128]{1,0:T(8,128)S(1)}, f32[8,128]{1,0:T(8,128)S(1)}, u32[]{:S(2)}, u32[]{:S(2)}) collective-permute-start(f32[8,128]{1,0:T(8,128)S(1)} %reduce_sum.9.mass_ref), channel_id=1, source_target_pairs={{0,3},{1,0},{2,1},{3,2},{4,7},{5,4},{6,5},{7,6},{8,11},{9,8},{10,9... | collective-permute-start | bytes 12296 | tf_op jit(solution)/shard_map/ppermute | solution.py:334
  127.4 13.3 %all-to-all-start.2 = ((f32[32,8,128]{2,1,0:T(8,128)}), f32[32,8,128]{2,1,0:T(8,128)S(1)}, u32[]{:S(2)}, u32[]{:S(2)}) async-start(f32[32,8,128]{2,1,0:T(8,128)} %broadcast_in_dim.10), calls=%async_computation.2 | async-start | bytes 262144 | tf_op jit(solution)/shard_map/all_to_all | solution.py:329
